TPU v7x, 512 devices: a whole 4x8x8 slice. The times are simulated.
512 devices in a mesh: cfg: 2 (over x_hi), uly: 8 (over y), blk: 32 (over z, x_lo, core).
Axes of the slice: x: 4 (x_hi: 2, x_lo: 2; x = x_hi * 2 + x_lo), y: 8, z: 8, core: 2. Of those that a mesh axis runs over, the one named last changes fastest.
Arguments:
- query_tokens: bfloat16 [2, 8192, 3072], P('cfg', ('uly', 'blk')), may hold values from -8 to 8
- key_tokens: bfloat16 [2, 4096, 3072], P('cfg', ('uly', 'blk')), may hold values from -8 to 8
- value_tokens: bfloat16 [2, 4096, 3072], P('cfg', ('uly', 'blk')), may hold values from -6 to 6
Outputs:
- guided: bfloat16 [8192, 24, 128], P(('uly', 'blk'), None, 'cfg')
All inputs are finite; a program needn't handle non-finite values.
Results may differ from a plain program's by a relative error of at most 0.008.
Values may be sent and summed in bfloat16 or wider, within the bound.
A program may use at most 64 MiB of HBM per device.

v0:
```python
import math

import jax
import jax.numpy as jnp
from jax import lax
from jax.sharding import PartitionSpec as P

D = 3072
HD = 128


GUIDE = 6.0


def swapped(array, axis, distance):
    return lax.ppermute(array, axis, [(i, i ^ 1 << distance) for i in range(lax.axis_size(axis))])


def update(state_now, queries, keys_in, values_in):
    running_max, running_sum, weighted = state_now
    scaling = 1.0 / math.sqrt(queries.shape[-1])
    logits = (
        jnp.einsum("qhd,khd->qhk", queries, keys_in, preferred_element_type=jnp.float32) * scaling
    )
    new_max = jnp.maximum(running_max, jnp.max(logits, axis=-1))
    exp_terms = jnp.exp(logits - new_max[..., None])
    running_sum = jnp.sum(exp_terms, axis=-1)
    weighted = jnp.einsum(
        "qhk,khd->qhd",
        exp_terms.astype(jnp.bfloat16),
        values_in,
        preferred_element_type=jnp.float32,
    )
    return (new_max, running_sum, weighted)


def local(query_tokens, key_tokens, value_tokens):
    head_size = HD
    half_size = head_size // 2
    head_count = D // head_size
    query_heads = query_tokens[0].reshape(query_tokens.shape[1], head_count, head_size)
    key_heads = key_tokens[0].reshape(key_tokens.shape[1], head_count, head_size)
    value_heads = value_tokens[0].reshape(value_tokens.shape[1], head_count, head_size)
    group_q, group_k, group_v = (
        lax.all_to_all(query_heads, "uly", split_axis=1, concat_axis=0, tiled=True),
        lax.all_to_all(key_heads, "uly", split_axis=1, concat_axis=0, tiled=True),
        lax.all_to_all(value_heads, "uly", split_axis=1, concat_axis=0, tiled=True),
    )
    q_rows = group_q.shape[0]
    local_heads = group_q.shape[1]
    initial = (
        jnp.full((q_rows, local_heads), -1e30, jnp.float32),
        jnp.zeros((q_rows, local_heads), jnp.float32),
        jnp.zeros((q_rows, local_heads, head_size), jnp.float32),
    )
    running_max, running_sum, weighted = update(
        initial,
        group_q,
        lax.all_gather(group_k, "blk", axis=0, tiled=True),
        lax.all_gather(group_v, "blk", axis=0, tiled=True),
    )
    attended = (weighted / running_sum[..., None]).astype(jnp.bfloat16)
    branch_index = lax.axis_index("cfg")
    is_cond = branch_index == 0
    own_start = branch_index * half_size
    other_start = (1 - branch_index) * half_size
    local_out = lax.all_to_all(attended, "uly", split_axis=0, concat_axis=1, tiled=True)
    outgoing = lax.dynamic_slice_in_dim(local_out, other_start, half_size, 2)
    partner = swapped(outgoing, "cfg", 0)
    own_half = lax.dynamic_slice_in_dim(local_out, own_start, half_size, 2)
    conditional = jnp.where(is_cond, own_half, partner).astype(jnp.float32)
    unconditional = jnp.where(is_cond, partner, own_half).astype(jnp.float32)
    return (unconditional + GUIDE * (conditional - unconditional)).astype(jnp.bfloat16)


def solution(mesh):
    in_specs = (
        P("cfg", ("uly", "blk"), None),
        P("cfg", ("uly", "blk"), None),
        P("cfg", ("uly", "blk"), None),
    )
    out_specs = P(("uly", "blk"), None, "cfg")
    return jax.shard_map(local, mesh=mesh, in_specs=in_specs, out_specs=out_specs, check_vma=False)
```

profile of v0, /device:TPU:1, one launch (start us, length us, event | category | flops | bytes accessed | tf_op | source)
XLA Modules:
  0.0 208.5 jit_solution(3309236034432374614)
XLA Ops:
  6.5 0.0 all-gather.3.cloned.1.call-start
  6.5 0.9 copy.42
  7.5 15.1 %all_to_all.72 = bf16[16,24,128]{2,0,1:T(8,128)(2,1)S(1)} all-to-all(bf16[16,24,128]{2,0,1:T(8,128)(2,1)S(1)} %copy.30), channel_id=1, replica_groups=mesh['cfg'=2,'uly'=8,'blk'=32] {'uly'}, dimensions={1} | all-to-all | bytes 196608 | tf_op jit(solution)/shard_map/all_to_all | solution.py:46
  22.6 0.6 copy.31
  23.2 0.0 all-gather.3.cloned.1.call-update
  23.2 0.0 all-gather.5.cloned.1.call-start
  23.3 0.9 copy.44
  24.2 10.1 %all_to_all.73 = bf16[16,24,128]{2,0,1:T(8,128)(2,1)S(1)} all-to-all(bf16[16,24,128]{2,0,1:T(8,128)(2,1)S(1)} %copy.34), channel_id=1, replica_groups=mesh['cfg'=2,'uly'=8,'blk'=32] {'uly'}, dimensions={1} | all-to-all | bytes 196608 | tf_op jit(solution)/shard_map/all_to_all | solution.py:47
  34.3 0.6 copy.35
  34.9 0.0 all-gather.5.cloned.1.call-update
  35.0 1.0 copy.43
  36.0 11.1 %all_to_all.74 = bf16[32,24,128]{2,0,1:T(8,128)(2,1)S(1)} all-to-all(bf16[32,24,128]{2,0,1:T(8,128)(2,1)S(1)} %copy.32), channel_id=1, replica_groups=mesh['cfg'=2,'uly'=8,'blk'=32] {'uly'}, dimensions={1} | all-to-all | bytes 393216 | tf_op jit(solution)/shard_map/all_to_all | solution.py:45
  47.1 46.6 %all-gather.3.cloned.1.call-done = bf16[4096,3,128]{2,0,1:T(8,128)(2,1)} async-done(((bf16[128,3,128]{2,0,1:T(8,128)(2,1)}), bf16[4096,3,128]{2,0,1:T(8,128)(2,1)}) %all-gather.3.cloned.1.call-update) | async-done | bytes 3145744 | tf_op jit(solution)/shard_map/all_gather | solution.py:59
  93.7 3.7 %bitcast_reduce_fusion = (f32[256,3]{0,1:T(4,128)S(1)}, f32[3,4096,256]{2,1,0:T(8,128)S(1)}) fusion(bf16[4096,3,128]{2,0,1:T(8,128)(2,1)} %all-gather.3.cloned.1.call-done, bf16[256,3,128]{2,0,1:T(8,128)(2,1)S(1)} %bitcast.52), kind=kOutput, calls=%fused_computation.1 | convolution fusion | flops 811597056 | bytes 15928320 | tf_op jit(solution)/shard_map/qhd,khd->qhk/dot_general | solution.py:23
  97.4 0.0 copy-start
  97.4 4.5 %copy-done = f32[3,4096,256]{2,1,0:T(8,128)} copy-done((f32[3,4096,256]{2,1,0:T(8,128)}, f32[3,4096,256]{2,1,0:T(8,128)S(1)}, u32[]{:S(2)}) %copy-start) | copy-done | bytes 12582936
  102.0 2.1 fusion.1
  104.0 60.3 %all-gather.5.cloned.1.call-done = bf16[4096,3,128]{2,0,1:T(8,128)(2,1)} async-done(((bf16[128,3,128]{2,0,1:T(8,128)(2,1)}), bf16[4096,3,128]{2,0,1:T(8,128)(2,1)}) %all-gather.5.cloned.1.call-update) | async-done | bytes 3145744 | tf_op jit(solution)/shard_map/all_gather | solution.py:60
  164.3 8.4 %fusion.13 = bf16[256,3,128]{2,0,1:T(8,128)(2,1)S(1)} fusion(bf16[4096,3,128]{2,0,1:T(8,128)(2,1)} %all-gather.5.cloned.1.call-done, f32[3,4096,256]{2,1,0:T(8,128)} %copy-done, f32[256,3]{0,1:T(4,128)S(1)} %broadcast_maximum_fusion, f32[256,3]{0,1:T(4,128)S(1)} %fusion.1), kind=kOutput, calls=%fused_computation.10 | convolution fusion | flops 814940160 | bytes 15931392 | tf_op jit(solution)/shard_map/qhk,khd->qhd/dot_general | solution.py:28
  172.7 0.9 copy.37
  173.6 6.5 %all-to-all-start.3 = ((bf16[256,3,128]{2,1,0:T(4,128)(2,1)}), bf16[256,3,128]{2,1,0:T(4,128)(2,1)S(1)}, u32[]{:S(2)}, u32[]{:S(2)}) async-start(bf16[256,3,128]{2,1,0:T(4,128)(2,1)} %copy.37), calls=%async_computation.3 | async-start | bytes 524288 | tf_op jit(solution)/shard_map/all_to_all | solution.py:67
  180.1 11.8 %all-to-all-done.3 = bf16[256,3,128]{2,1,0:T(4,128)(2,1)S(1)} async-done(((bf16[256,3,128]{2,1,0:T(4,128)(2,1)}), bf16[256,3,128]{2,1,0:T(4,128)(2,1)S(1)}, u32[]{:S(2)}, u32[]{:S(2)}) %all-to-all-start.3) | async-done | bytes 196640 | tf_op jit(solution)/shard_map/all_to_all | solution.py:67
  191.9 0.1 constant_dynamic-slice_fusion
  192.0 4.2 %collective-permute-start = (bf16[32,24,64]{2,0,1:T(8,128)(2,1)S(1)}, bf16[32,24,64]{2,0,1:T(8,128)(2,1)S(1)}, u32[]{:S(2)}, u32[]{:S(2)}) collective-permute-start(bf16[32,24,64]{2,0,1:T(8,128)(2,1)S(1)} %constant_dynamic-slice_fusion), channel_id=1, source_target_pairs={{0,256},{256,0},{1,257},{257,1},{2,258},{258,2},{3,259},{259,3},{4... | collective-permute-start | bytes 294920 | tf_op jit(solution)/shard_map/ppermute | solution.py:16
  196.3 4.5 %collective-permute-done = bf16[32,24,64]{2,0,1:T(8,128)(2,1)S(1)} collective-permute-done((bf16[32,24,64]{2,0,1:T(8,128)(2,1)S(1)}, bf16[32,24,64]{2,0,1:T(8,128)(2,1)S(1)}, u32[]{:S(2)}, u32[]{:S(2)}) %collective-permute-start) | collective-permute-done | bytes 98336 | tf_op jit(solution)/shard_map/ppermute | solution.py:16
  200.7 0.2 fusion.17
  200.9 0.8 copy.40
  (7 shorter events, 0.1 us)
Async XLA Ops:
  6.5 87.2 %all-gather.3.cloned.1.call-start = ((), (), s32[]{:S(2)}) async-start(), calls=%async_computation.4 | async-start | bytes 3244032 | tf_op jit(solution)/shard_map/all_gather | solution.py:59
  23.2 141.1 %all-gather.5.cloned.1.call-start = ((), (), s32[]{:S(2)}) async-start(), calls=%async_computation.5 | async-start | bytes 3244032 | tf_op jit(solution)/shard_map/all_gather | solution.py:60
  97.4 4.5 %copy-start = (f32[3,4096,256]{2,1,0:T(8,128)}, f32[3,4096,256]{2,1,0:T(8,128)S(1)}, u32[]{:S(2)}) copy-start(f32[3,4096,256]{2,1,0:T(8,128)S(1)} %get-tuple-element.6) | copy-start | bytes 37748740
  173.6 18.2 %all-to-all-start.3 = ((bf16[256,3,128]{2,1,0:T(4,128)(2,1)}), bf16[256,3,128]{2,1,0:T(4,128)(2,1)S(1)}, u32[]{:S(2)}, u32[]{:S(2)}) async-start(bf16[256,3,128]{2,1,0:T(4,128)(2,1)} %copy.37), calls=%async_computation.3 | async-start | bytes 524288 | tf_op jit(solution)/shard_map/all_to_all | solution.py:67
  192.0 8.7 %collective-permute-start = (bf16[32,24,64]{2,0,1:T(8,128)(2,1)S(1)}, bf16[32,24,64]{2,0,1:T(8,128)(2,1)S(1)}, u32[]{:S(2)}, u32[]{:S(2)}) collective-permute-start(bf16[32,24,64]{2,0,1:T(8,128)(2,1)S(1)} %constant_dynamic-slice_fusion), channel_id=1, source_target_pairs={{0,256},{256,0},{1,257},{257,1},{2,258},{258,2},{3,259},{259,3},{4... | collective-permute-start | bytes 294920 | tf_op jit(solution)/shard_map/ppermute | solution.py:16
Sparse Core Ops, SparseCore 0:
  23.4 70.2 all-gather.2
  95.9 68.4 all-gather.4
where the time goes:
time: 209 us
  waiting for transfers between devices  123 us (59%)
  blocking collectives  36.3 us (17%)
  between operations  13.5 us (6%)
  matrix products  12.1 us (6%)
  starting transfers between devices  10.7 us (5%)
  local copies, waits for them, and re-layouts  10.4 us (5%)
  other arithmetic  2.25 us (1%)
    all_gather x1, waiting for transfers between devices, local(): lax.all_gather(group_v, 'blk', axis=0, tiled=True)  60.3 us
    all_gather x1, waiting for transfers between devices, local(): lax.all_gather(group_k, 'blk', axis=0, tiled=True)  46.6 us
    all_to_all x1, blocking collectives, local(): lax.all_to_all(key_heads, 'uly', split_axis=1, concat_axis=0, tiled=True)  15.1 us
    all_to_all x1, waiting for transfers between devices, local(): lax.all_to_all(attended, 'uly', split_axis=0, concat_axis=1, tiled=True)  11.8 us
    all_to_all x1, blocking collectives, local(): lax.all_to_all(query_heads, 'uly', split_axis=1, concat_axis=0, tiled=True)  11.1 us
    all_to_all x1, blocking collectives, local(): lax.all_to_all(value_heads, 'uly', split_axis=1, concat_axis=0, tiled=True)  10.1 us
    dot_general x1, matrix products, update(): jnp.einsum('qhk,khd->qhd', exp_terms.astype(jnp.bfloat16), values_in, pre...  8.41 us
    unnamed x5, local copies, waits for them, and re-layouts  7.3 us
  transfers between devices with their start and end apart: 4, of which 4 were waited for; matrix products, arithmetic and copies ran while one was open for 4% of the time, Pallas kernels for 0%

commit v1 on v0

v1 whole, which is shorter than its diff:
```python
import functools
import math

import jax
import jax.numpy as jnp
from jax import lax
from jax.experimental import pallas as pl
from jax.experimental.pallas import tpu as pltpu
from jax.sharding import PartitionSpec as P

GUIDE = 6.0
HD = 128
HEADS = 24
RING = 8
LOG2E = math.log2(math.e)
SCALE = LOG2E / math.sqrt(HD)
MESH = pl.DeviceIdType.MESH
F32 = jnp.float32
BF16 = jnp.bfloat16


def kernel(
    q_in, k_in, v_in, out,
    kv, q, acc, top, o_send, o_got,
    kv_got, q_got, ring_got, core_got, out_got,
    a2a_sent, edge_sent, ring_sent, core_sent, out_sent,
):
    c = lax.axis_index("cfg")
    y = lax.axis_index("uly")
    blk = lax.axis_index("blk")
    z = lax.div(blk, 4)
    xl = lax.rem(lax.div(blk, 2), 2)
    core = lax.rem(blk, 2)

    def device(c_, y_, z_, xl_, core_):
        return (c_, y_, z_ * 4 + xl_ * 2 + core_)

    def place(t, a_, r_, xl_, c_=c):
        return device(c_, a_, r_, xl_, core) if t == 0 else device(c_, r_, a_, xl_, core)

    at = (y, z)
    along = (z, y)
    apart = [xl if t == 0 else 1 - xl for t in range(2)]
    odd = [lax.rem(at[t], 2) for t in range(2)]
    active = [jnp.logical_or(apart[t] == 0, odd[t] == 0) for t in range(2)]
    head = [12 * t + jnp.where(apart[t] == 0, at[t], 8 + lax.div(at[t], 2)) for t in range(2)]
    mate = device(c, y, z, xl, 1 - core)

    def turn(a, j):
        return lax.rem(a + j, RING)

    barrier = pltpu.get_barrier_semaphore()
    peers = [mate, device(1 - c, y, z, xl, core), device(c, y, z, 1 - xl, core)]
    for j in range(1, RING):
        for x_ in (xl, 1 - xl):
            peers.append(device(c, turn(y, j), z, x_, core))
            peers.append(device(c, y, turn(z, j), x_, core))
    for p in peers:
        pl.semaphore_signal(barrier, inc=1, device_id=p, device_id_type=MESH)
    pl.semaphore_wait(barrier, len(peers))

    def targets(t):
        a = at[t]
        result = []
        for j in range(RING):
            to = turn(a, j)
            slot = ((RING - j) % RING) * 2 + apart[t]
            result.append((to, t, 12 * t + to, slot, (apart[t] == 0) if j == 0 else None))
        pair = lax.div(a, 2)
        for j in range(4):
            to = 2 * lax.rem(pair + j, 4)
            slot = lax.rem(a - to + RING, RING) * 2 + (1 - apart[t])
            here = jnp.logical_and(apart[t] == 1, odd[t] == 0) if j == 0 else None
            result.append((to, 1 - t, 12 * t + 8 + lax.div(to, 2), slot, here))
        return result

    def columns(h):
        return pl.ds(pl.multiple_of(h * HD, HD), HD)

    def send_piece(src, dst, sent, got, target, here, where, edge):
        def remote(sem):
            pltpu.make_async_remote_copy(
                src_ref=src, dst_ref=dst, send_sem=sem, recv_sem=got,
                device_id=target, device_id_type=MESH,
            ).start()

        if here is None:
            remote(sent)
            return

        @pl.when(here)
        def _():
            pltpu.make_async_copy(src, dst, got).start()

        @pl.when(jnp.logical_not(here))
        def _():
            remote(edge)

    where = [targets(0), targets(1)]
    for i in range(12):
        for part, ref in enumerate((k_in, v_in)):
            for t in range(2):
                to, x_, h, slot, here = where[t][i]
                send_piece(
                    ref.at[0, :, columns(h)], kv.at[t, 0, 0, part, slot],
                    a2a_sent.at[t], kv_got.at[t, part], place(t, to, along[t], x_), here,
                    where, edge_sent.at[t, 0 if i == 0 else 1],
                )
    for i in range(12):
        for t in range(2):
            to, x_, h, slot, here = where[t][i]
            send_piece(
                q_in.at[0, :, columns(h)], q.at[t, slot],
                a2a_sent.at[t], q_got.at[t], place(t, to, along[t], x_), here,
                where, edge_sent.at[t, 0 if i == 0 else 1],
            )

    def await_bytes(ref, sem):
        pltpu.make_async_copy(ref, ref, sem).wait()

    def pass_on(t, r, part):
        piece = kv.at[t, r, 0, part]
        ahead = r in (0, 7, 6) or (r == 5 and part == 0)
        back = r in (0, 1, 2) or (r == 3 and part == 1)
        for go, step in ((ahead, 1), (back, 7)):
            if go:
                there = (r - step) % RING
                pltpu.make_async_remote_copy(
                    src_ref=piece, dst_ref=kv.at[t, there, 0, part],
                    send_sem=ring_sent.at[t], recv_sem=ring_got.at[t, there, part],
                    device_id=place(t, at[t], turn(along[t], step), xl),
                    device_id_type=MESH,
                ).start()
        pltpu.make_async_remote_copy(
            src_ref=piece, dst_ref=kv.at[t, r, 1, part],
            send_sem=core_sent.at[t], recv_sem=core_got.at[t, r, part],
            device_id=mate, device_id_type=MESH,
        ).start()

    def relay(t, *offsets):
        for r, part in [(r, part) for r in offsets for part in range(2)]:
            if r == 0:
                await_bytes(kv.at[t, 0, 0, part], kv_got.at[t, part])
            else:
                await_bytes(kv.at[t, r, 0, part], ring_got.at[t, r, part])
            pass_on(t, r, part)

    def attend(t, offsets, first):
        for r in offsets:
            for part in range(2):
                await_bytes(kv.at[t, r, 1, part], core_got.at[t, r, part])
        ones = jnp.ones((256, HD), BF16)
        for b in range(2):
            rows = q[t, 8 * b : 8 * b + 8].reshape(256, HD)
            span = pl.ds(256 * b, 256)
            logits = [
                lax.dot_general(
                    rows, kv[t, r, w, 0].reshape(256, HD), (((1,), (1,)), ((), ())),
                    preferred_element_type=F32,
                )
                for r in offsets
                for w in range(2)
            ]
            peak = logits[0]
            for s in logits[1:]:
                peak = jnp.maximum(peak, s)
            peak = jnp.max(peak, axis=1, keepdims=True) * SCALE
            if not first:
                before = top[t, span, 0:1]
                peak = jnp.maximum(before, peak)
            total = None
            for i, (r, w) in enumerate([(r, w) for r in offsets for w in range(2)]):
                weights = jnp.exp2(logits[i] * SCALE - peak).astype(BF16)
                values = jnp.concatenate([kv[t, r, w, 1].reshape(256, HD), ones], axis=1)
                term = jnp.dot(weights, values, preferred_element_type=F32)
                total = term if total is None else total + term
            if not first:
                total = total + acc[t, span] * jnp.exp2(before - peak)
            acc[t, span] = total
            top[t, span] = jnp.broadcast_to(peak, (256, HD))

    def both(f, *args):
        for t in range(2):
            pl.when(active[t])(functools.partial(f, t, *args))

    both(relay, 0)
    both(lambda t: await_bytes(q.at[t], q_got.at[t]))
    both(relay, 1, 7)
    both(attend, (0,), True)
    both(relay, 2, 6)
    both(attend, (1, 7), False)
    both(relay, 3, 5)
    both(attend, (2, 6), False)
    both(relay, 4)
    both(attend, (3, 5), False)

    def finish(t):
        attend(t, (4,), False)
        whole = acc[t]
        result = (whole[:, :HD] / whole[:, HD:]).reshape(16, 2, 16, HD)
        upper, lower = result[:, 0].reshape(256, HD), result[:, 1].reshape(256, HD)
        left = lax.broadcasted_iota(jnp.int32, (256, HD), 1) < 64
        o_send[t, 0] = jnp.where(left, upper, pltpu.roll(lower, 64, 1)).astype(BF16).reshape(16, 16, HD)
        o_send[t, 1] = jnp.where(left, pltpu.roll(upper, 64, 1), lower).astype(BF16).reshape(16, 16, HD)
        for j in range(RING):
            for b in range(2):
                for other in range(2):
                    c_ = c if other == 0 else 1 - c
                    x_ = xl if b == 0 else 1 - xl
                    src = o_send.at[t, c_, 2 * j + b]
                    dst = o_got.at[head[t], c]
                    if j == b == other == 0:
                        pltpu.make_async_copy(src, dst, out_got.at[0]).start()
                        continue
                    pltpu.make_async_remote_copy(
                        src_ref=src, dst_ref=dst,
                        send_sem=out_sent.at[t], recv_sem=out_got.at[0],
                        device_id=place(t, turn(at[t], j), along[t], x_, c_),
                        device_id_type=MESH,
                    ).start()

    both(finish)

    for t in range(2):
        await_bytes(kv.at[t, pl.ds(0, 5), 0, 0, pl.ds(0, 8)], a2a_sent.at[t])
        for e, (i, here) in enumerate(((0, where[t][0][4]), (8, where[t][8][4]))):
            @pl.when(jnp.logical_not(here))
            def _(t=t, e=e):
                await_bytes(kv.at[t, 0, 0, 0, pl.ds(0, 4)], edge_sent.at[t, e])

    def drain(t):
        await_bytes(kv.at[t, pl.ds(0, 7), 0], ring_sent.at[t])
        await_bytes(kv.at[t, :, 0], core_sent.at[t])
        await_bytes(kv.at[t, 0, 0, 0, pl.ds(0, 15)], out_sent.at[t])
        await_bytes(kv.at[t, 0, 0, 0], out_sent.at[t])

    await_bytes(o_got, out_got.at[0])
    conditional, unconditional = o_got[:, 0].astype(F32), o_got[:, 1].astype(F32)
    out[...] = (unconditional + GUIDE * (conditional - unconditional)).astype(BF16)
    both(drain)


def local(query_tokens, key_tokens, value_tokens):
    anywhere = pl.BlockSpec(memory_space=pl.ANY)
    dma = pltpu.SemaphoreType.DMA
    guided = pl.pallas_call(
        kernel,
        out_shape=jax.ShapeDtypeStruct((HEADS, 16, HD), BF16),
        in_specs=[anywhere] * 3,
        out_specs=pl.BlockSpec(memory_space=pltpu.VMEM),
        scratch_shapes=[
            pltpu.VMEM((2, RING, 2, 2, 16, 16, HD), BF16),
            pltpu.VMEM((2, 16, 32, HD), BF16),
            pltpu.VMEM((2, 512, 2 * HD), F32),
            pltpu.VMEM((2, 512, HD), F32),
            pltpu.VMEM((2, 2, 16, 16, HD), BF16),
            pltpu.VMEM((HEADS, 2, 16, HD), BF16),
            dma((2, 2)), dma((2,)), dma((2, RING, 2)), dma((2, RING, 2)), dma((1,)),
            dma((2,)), dma((2, 2)), dma((2,)), dma((2,)), dma((2,)),
        ],
        compiler_params=pltpu.CompilerParams(
            collective_id=0, has_side_effects=True, vmem_limit_bytes=48 << 20
        ),
        name="guided_attention",
    )(query_tokens, key_tokens, value_tokens)
    halves = guided.reshape(HEADS, 16, 2, HD // 2)
    return halves.transpose(2, 1, 0, 3).reshape(32, HEADS, HD // 2)


def solution(mesh):
    tokens = P("cfg", ("uly", "blk"), None)
    return jax.shard_map(
        local, mesh=mesh, in_specs=(tokens,) * 3,
        out_specs=P(("uly", "blk"), None, "cfg"), check_vma=False,
    )
```

time: 209 us -> 55.5 us (0.27)
  the two profiles are of different devices: /device:TPU:1 before, /device:TPU:2 now
where the time goes in v1:
time: 55.5 us; the launch traced here: 55.3 us
  Pallas kernels  51.7 us (93%)
  local copies, waits for them, and re-layouts  3.59 us (6%)
    pallas_call x1, Pallas kernels, local(): pl.pallas_call(kernel, out_shape=jax.ShapeDtypeStruct((HEADS, 16, HD), BF...  51.7 us
    unnamed x6, local copies, waits for them, and re-layouts  2.71 us

profile of v1, /device:TPU:2, one launch (start us, length us, event | category | flops | bytes accessed | tf_op | source)
XLA Modules:
  0.0 55.3 jit_solution(16814811734958036071)
XLA Ops:
  0.0 0.0 copy-start
  0.0 0.9 %copy-done = bf16[1,32,3072]{2,1,0:T(8,128)(2,1)S(1)} copy-done((bf16[1,32,3072]{2,1,0:T(8,128)(2,1)S(1)}, bf16[1,32,3072]{2,1,0:T(8,128)(2,1)}, u32[]{:S(2)}) %copy-start) | copy-done | bytes 196632
  0.9 0.0 copy-start.1
  0.9 0.9 %copy-done.1 = bf16[1,16,3072]{2,1,0:T(8,128)(2,1)S(1)} copy-done((bf16[1,16,3072]{2,1,0:T(8,128)(2,1)S(1)}, bf16[1,16,3072]{2,1,0:T(8,128)(2,1)}, u32[]{:S(2)}) %copy-start.1) | copy-done | bytes 98328
  1.8 0.0 copy-start.2
  1.8 0.9 %copy-done.2 = bf16[1,16,3072]{2,1,0:T(8,128)(2,1)S(1)} copy-done((bf16[1,16,3072]{2,1,0:T(8,128)(2,1)S(1)}, bf16[1,16,3072]{2,1,0:T(8,128)(2,1)}, u32[]{:S(2)}) %copy-start.2) | copy-done | bytes 98328
  2.7 51.7 %guided_attention.1 = bf16[24,16,128]{2,1,0:T(8,128)(2,1)S(1)} custom-call(bf16[1,32,3072]{2,1,0:T(8,128)(2,1)S(1)} %copy-done, bf16[1,16,3072]{2,1,0:T(8,128)(2,1)S(1)} %copy-done.1, bf16[1,16,3072]{2,1,0:T(8,128)(2,1)S(1)} %copy-done.2), custom_call_target="tpu_custom_call" | custom-call | tf_op jit(solution)/shard_map/guided_attention/pallas_call | solution.py:246
  54.4 0.1 reshape.6
  54.5 0.8 %copy.4 = bf16[2,16,24,64]{3,2,1,0:T(8,128)(2,1)} copy(bf16[2,16,24,64]{3,0,1,2:T(2,128)(2,1)S(1)} %bitcast.2) | data formatting | bytes 196608 | tf_op jit(solution)/shard_map/transpose | solution.py:267
Async XLA Ops:
  0.0 0.9 %copy-start = (bf16[1,32,3072]{2,1,0:T(8,128)(2,1)S(1)}, bf16[1,32,3072]{2,1,0:T(8,128)(2,1)}, u32[]{:S(2)}) copy-start(bf16[1,32,3072]{2,1,0:T(8,128)(2,1)} %q_in.1) | copy-start | bytes 589828
  0.9 0.9 %copy-start.1 = (bf16[1,16,3072]{2,1,0:T(8,128)(2,1)S(1)}, bf16[1,16,3072]{2,1,0:T(8,128)(2,1)}, u32[]{:S(2)}) copy-start(bf16[1,16,3072]{2,1,0:T(8,128)(2,1)} %k_in.1) | copy-start | bytes 294916
  1.8 0.9 %copy-start.2 = (bf16[1,16,3072]{2,1,0:T(8,128)(2,1)S(1)}, bf16[1,16,3072]{2,1,0:T(8,128)(2,1)}, u32[]{:S(2)}) copy-start(bf16[1,16,3072]{2,1,0:T(8,128)(2,1)} %v_in.1) | copy-start | bytes 294916

commit v2 on v1

--- a/solution.py
+++ b/solution.py
@@ -9,6 +9,8 @@
 from jax.sharding import PartitionSpec as P
 
 GUIDE = 6.0
+FAR_FIRST = (4, 3, 5, 2, 6, 1, 7, 0)
+SENDS = (4, 10, 3, 5, 9, 11, 2, 6, 8, 1, 7, 0)
 HD = 128
 HEADS = 24
 RING = 8
@@ -21,8 +23,8 @@
 
 def kernel(
     q_in, k_in, v_in, out,
-    kv, q, acc, top, o_send, o_got,
-    kv_got, q_got, ring_got, core_got, out_got,
+    kv_out, q_out, kv, q, acc, top, o_send, o_got, spread,
+    staged,    kv_got, q_got, ring_got, core_got, out_got,
     a2a_sent, edge_sent, ring_sent, core_sent, out_sent,
 ):
     c = lax.axis_index("cfg")
@@ -51,12 +53,24 @@
 
     barrier = pltpu.get_barrier_semaphore()
     peers = [mate, device(1 - c, y, z, xl, core), device(c, y, z, 1 - xl, core)]
-    for j in range(1, RING):
+    for j in FAR_FIRST[:-1]:
         for x_ in (xl, 1 - xl):
             peers.append(device(c, turn(y, j), z, x_, core))
             peers.append(device(c, y, turn(z, j), x_, core))
     for p in peers:
         pl.semaphore_signal(barrier, inc=1, device_id=p, device_id_type=MESH)
+    def columns(h):
+        return pl.ds(h * HD, HD)
+
+    for h in range(HEADS):
+        for part, ref in enumerate((k_in, v_in)):
+            pltpu.make_async_copy(ref.at[0, :, columns(h)], kv_out.at[h, part], staged.at[0]).start()
+    for h in range(HEADS):
+        pltpu.make_async_copy(q_in.at[0, :, columns(h)], q_out.at[h], staged.at[1]).start()
+
+    def await_bytes(ref, sem):
+        pltpu.make_async_copy(ref, ref, sem).wait()
+
     pl.semaphore_wait(barrier, len(peers))
 
     def targets(t):
@@ -74,10 +88,7 @@
             result.append((to, 1 - t, 12 * t + 8 + lax.div(to, 2), slot, here))
         return result
 
-    def columns(h):
-        return pl.ds(pl.multiple_of(h * HD, HD), HD)
-
-    def send_piece(src, dst, sent, got, target, here, where, edge):
+    def send_piece(src, dst, sent, got, target, here, edge):
         def remote(sem):
             pltpu.make_async_remote_copy(
                 src_ref=src, dst_ref=dst, send_sem=sem, recv_sem=got,
@@ -97,26 +108,24 @@
             remote(edge)
 
     where = [targets(0), targets(1)]
-    for i in range(12):
-        for part, ref in enumerate((k_in, v_in)):
-            for t in range(2):
-                to, x_, h, slot, here = where[t][i]
-                send_piece(
-                    ref.at[0, :, columns(h)], kv.at[t, 0, 0, part, slot],
-                    a2a_sent.at[t], kv_got.at[t, part], place(t, to, along[t], x_), here,
-                    where, edge_sent.at[t, 0 if i == 0 else 1],
-                )
-    for i in range(12):
+    await_bytes(kv_out, staged.at[0])
+    for i in SENDS:
         for t in range(2):
             to, x_, h, slot, here = where[t][i]
             send_piece(
-                q_in.at[0, :, columns(h)], q.at[t, slot],
+                kv_out.at[h], kv.at[t, 0, 0, :, slot],
+                a2a_sent.at[t], kv_got.at[t], place(t, to, along[t], x_), here,
+                edge_sent.at[t, 0 if i == 0 else 1],
+            )
+    await_bytes(q_out, staged.at[1])
+    for i in SENDS:
+        for t in range(2):
+            to, x_, h, slot, here = where[t][i]
+            send_piece(
+                q_out.at[h], q.at[t, slot],
                 a2a_sent.at[t], q_got.at[t], place(t, to, along[t], x_), here,
-                where, edge_sent.at[t, 0 if i == 0 else 1],
+                edge_sent.at[t, 0 if i == 0 else 1],
             )
-
-    def await_bytes(ref, sem):
-        pltpu.make_async_copy(ref, ref, sem).wait()
 
     def pass_on(t, r, part):
         piece = kv.at[t, r, 0, part]
@@ -137,61 +146,71 @@
             device_id=mate, device_id_type=MESH,
         ).start()
 
-    def relay(t, *offsets):
-        for r, part in [(r, part) for r in offsets for part in range(2)]:
-            if r == 0:
-                await_bytes(kv.at[t, 0, 0, part], kv_got.at[t, part])
-            else:
-                await_bytes(kv.at[t, r, 0, part], ring_got.at[t, r, part])
-            pass_on(t, r, part)
+    def relay(*offsets):
+        for part in range(2):
+            for t in range(2):
+                @pl.when(active[t])
+                def _(t=t, part=part):
+                    for r in offsets:
+                        if r != 0:
+                            await_bytes(kv.at[t, r, 0, part], ring_got.at[t, r, part])
+                        elif part == 0:
+                            await_bytes(kv.at[t, 0, 0], kv_got.at[t])
+                        pass_on(t, r, part)
 
     def attend(t, offsets, first):
         for r in offsets:
             for part in range(2):
                 await_bytes(kv.at[t, r, 1, part], core_got.at[t, r, part])
         ones = jnp.ones((256, HD), BF16)
-        for b in range(2):
+        chunks = [(r, w) for r in offsets for w in range(2)]
+
+        def score(b):
             rows = q[t, 8 * b : 8 * b + 8].reshape(256, HD)
-            span = pl.ds(256 * b, 256)
-            logits = [
+            return [
                 lax.dot_general(
                     rows, kv[t, r, w, 0].reshape(256, HD), (((1,), (1,)), ((), ())),
                     preferred_element_type=F32,
                 )
-                for r in offsets
-                for w in range(2)
+                for r, w in chunks
             ]
-            peak = logits[0]
-            for s in logits[1:]:
-                peak = jnp.maximum(peak, s)
+
+        def mix(b, logits):
+            span = pl.ds(256 * b, 256)
+            peak = functools.reduce(jnp.maximum, logits)
             peak = jnp.max(peak, axis=1, keepdims=True) * SCALE
             if not first:
                 before = top[t, span, 0:1]
                 peak = jnp.maximum(before, peak)
+            weights = [jnp.exp2(s * SCALE - peak) for s in logits]
             total = None
-            for i, (r, w) in enumerate([(r, w) for r in offsets for w in range(2)]):
-                weights = jnp.exp2(logits[i] * SCALE - peak).astype(BF16)
+            for p, (r, w) in zip(weights, chunks):
                 values = jnp.concatenate([kv[t, r, w, 1].reshape(256, HD), ones], axis=1)
-                term = jnp.dot(weights, values, preferred_element_type=F32)
+                term = jnp.dot(p.astype(BF16), values, preferred_element_type=F32)
                 total = term if total is None else total + term
             if not first:
                 total = total + acc[t, span] * jnp.exp2(before - peak)
             acc[t, span] = total
             top[t, span] = jnp.broadcast_to(peak, (256, HD))
 
+        upper = score(0)
+        lower = score(1)
+        mix(0, upper)
+        mix(1, lower)
+
     def both(f, *args):
         for t in range(2):
             pl.when(active[t])(functools.partial(f, t, *args))
 
-    both(relay, 0)
+    relay(0)
     both(lambda t: await_bytes(q.at[t], q_got.at[t]))
-    both(relay, 1, 7)
+    relay(1, 7)
     both(attend, (0,), True)
-    both(relay, 2, 6)
+    relay(2, 6)
     both(attend, (1, 7), False)
-    both(relay, 3, 5)
+    relay(3, 5)
     both(attend, (2, 6), False)
-    both(relay, 4)
+    relay(4)
     both(attend, (3, 5), False)
 
     def finish(t):
@@ -202,9 +221,9 @@
         left = lax.broadcasted_iota(jnp.int32, (256, HD), 1) < 64
         o_send[t, 0] = jnp.where(left, upper, pltpu.roll(lower, 64, 1)).astype(BF16).reshape(16, 16, HD)
         o_send[t, 1] = jnp.where(left, pltpu.roll(upper, 64, 1), lower).astype(BF16).reshape(16, 16, HD)
-        for j in range(RING):
-            for b in range(2):
-                for other in range(2):
+        for j in FAR_FIRST:
+            for b in (1, 0):
+                for other in (1, 0):
                     c_ = c if other == 0 else 1 - c
                     x_ = xl if b == 0 else 1 - xl
                     src = o_send.at[t, c_, 2 * j + b]
@@ -235,36 +254,41 @@
         await_bytes(kv.at[t, 0, 0, 0], out_sent.at[t])
 
     await_bytes(o_got, out_got.at[0])
-    conditional, unconditional = o_got[:, 0].astype(F32), o_got[:, 1].astype(F32)
-    out[...] = (unconditional + GUIDE * (conditional - unconditional)).astype(BF16)
+    for h in range(HEADS):
+        conditional, unconditional = o_got[h, 0].astype(F32), o_got[h, 1].astype(F32)
+        guided = unconditional + GUIDE * (conditional - unconditional)
+        spread[pl.ds(h, 16, stride=HEADS), :] = guided
+        spread[pl.ds(16 * HEADS + h, 16, stride=HEADS), :] = pltpu.roll(guided, 64, 1)
+    out[...] = spread[...].reshape(32, HEADS, HD)[:, :, : HD // 2].astype(BF16)
     both(drain)
 
 
 def local(query_tokens, key_tokens, value_tokens):
-    anywhere = pl.BlockSpec(memory_space=pl.ANY)
+    anywhere = pl.BlockSpec(memory_space=pltpu.HBM)
     dma = pltpu.SemaphoreType.DMA
-    guided = pl.pallas_call(
+    return pl.pallas_call(
         kernel,
-        out_shape=jax.ShapeDtypeStruct((HEADS, 16, HD), BF16),
+        out_shape=jax.ShapeDtypeStruct((32, HEADS, HD // 2), BF16),
         in_specs=[anywhere] * 3,
         out_specs=pl.BlockSpec(memory_space=pltpu.VMEM),
         scratch_shapes=[
+            pltpu.VMEM((HEADS, 2, 16, HD), BF16),
+            pltpu.VMEM((HEADS, 32, HD), BF16),
             pltpu.VMEM((2, RING, 2, 2, 16, 16, HD), BF16),
             pltpu.VMEM((2, 16, 32, HD), BF16),
             pltpu.VMEM((2, 512, 2 * HD), F32),
             pltpu.VMEM((2, 512, HD), F32),
             pltpu.VMEM((2, 2, 16, 16, HD), BF16),
             pltpu.VMEM((HEADS, 2, 16, HD), BF16),
-            dma((2, 2)), dma((2,)), dma((2, RING, 2)), dma((2, RING, 2)), dma((1,)),
+            pltpu.VMEM((32 * HEADS, HD), F32),
+            dma((2,)), dma((2,)), dma((2,)), dma((2, RING, 2)), dma((2, RING, 2)), dma((1,)),
             dma((2,)), dma((2, 2)), dma((2,)), dma((2,)), dma((2,)),
         ],
         compiler_params=pltpu.CompilerParams(
-            collective_id=0, has_side_effects=True, vmem_limit_bytes=48 << 20
+            collective_id=0, has_side_effects=True, vmem_limit_bytes=64 * 2**20 - 2**16
         ),
         name="guided_attention",
     )(query_tokens, key_tokens, value_tokens)
-    halves = guided.reshape(HEADS, 16, 2, HD // 2)
-    return halves.transpose(2, 1, 0, 3).reshape(32, HEADS, HD // 2)
 
 
 def solution(mesh):

time: 55.5 us -> 51.1 us (0.921)
  the two profiles are of different devices: /device:TPU:2 before, /device:TPU:1 now
where the time goes in v2:
time: 51.1 us; the launch traced here: 50.6 us
  Pallas kernels  49 us (96%)
  local copies, waits for them, and re-layouts  1.62 us (3%)
    pallas_call x1, Pallas kernels, local(): pl.pallas_call(kernel, out_shape=jax.ShapeDtypeStruct((32, HEADS, HD // 2...  49 us
    unnamed x1, local copies, waits for them, and re-layouts  1.62 us

profile of v2, /device:TPU:1, one launch (start us, length us, event | category | flops | bytes accessed | tf_op | source)
XLA Modules:
  0.0 50.6 jit_solution(7137761829142670309)
XLA Ops:
  0.0 49.0 %guided_attention.1 = bf16[32,24,64]{2,1,0:T(8,128)(2,1)} custom-call(bf16[1,32,3072]{2,1,0:T(8,128)(2,1)} %q_in.1, bf16[1,16,3072]{2,1,0:T(8,128)(2,1)} %k_in.1, bf16[1,16,3072]{2,1,0:T(8,128)(2,1)} %v_in.1), custom_call_target="tpu_custom_call" | custom-call | tf_op jit(solution)/shard_map/guided_attention/pallas_call | solution.py:269
  49.0 1.6 %copy.5 = bf16[32,24,64]{2,1,0:T(8,128)(2,1)} copy(bf16[32,24,64]{2,1,0:T(8,128)(2,1)} %guided_attention.1) | data formatting | bytes 196608

commit v3 on v2

--- a/solution.py
+++ b/solution.py
@@ -44,7 +44,7 @@
     along = (z, y)
     apart = [xl if t == 0 else 1 - xl for t in range(2)]
     odd = [lax.rem(at[t], 2) for t in range(2)]
-    active = [jnp.logical_or(apart[t] == 0, odd[t] == 0) for t in range(2)]
+    active = [jnp.logical_or(apart[t] == 0, odd[t] == 1) for t in range(2)]
     head = [12 * t + jnp.where(apart[t] == 0, at[t], 8 + lax.div(at[t], 2)) for t in range(2)]
     mate = device(c, y, z, xl, 1 - core)
 
@@ -82,9 +82,9 @@
             result.append((to, t, 12 * t + to, slot, (apart[t] == 0) if j == 0 else None))
         pair = lax.div(a, 2)
         for j in range(4):
-            to = 2 * lax.rem(pair + j, 4)
+            to = 2 * lax.rem(pair + j, 4) + 1
             slot = lax.rem(a - to + RING, RING) * 2 + (1 - apart[t])
-            here = jnp.logical_and(apart[t] == 1, odd[t] == 0) if j == 0 else None
+            here = jnp.logical_and(apart[t] == 1, odd[t] == 1) if j == 0 else None
             result.append((to, 1 - t, 12 * t + 8 + lax.div(to, 2), slot, here))
         return result
 
@@ -204,14 +204,14 @@
 
     relay(0)
     both(lambda t: await_bytes(q.at[t], q_got.at[t]))
+    both(attend, (0,), True)
     relay(1, 7)
-    both(attend, (0,), True)
+    both(attend, (1, 7), False)
     relay(2, 6)
-    both(attend, (1, 7), False)
+    both(attend, (2, 6), False)
     relay(3, 5)
-    both(attend, (2, 6), False)
+    both(attend, (3, 5), False)
     relay(4)
-    both(attend, (3, 5), False)
 
     def finish(t):
         attend(t, (4,), False)
@@ -229,11 +229,11 @@
                     src = o_send.at[t, c_, 2 * j + b]
                     dst = o_got.at[head[t], c]
                     if j == b == other == 0:
-                        pltpu.make_async_copy(src, dst, out_got.at[0]).start()
+                        pltpu.make_async_copy(src, dst, out_got.at[t]).start()
                         continue
                     pltpu.make_async_remote_copy(
                         src_ref=src, dst_ref=dst,
-                        send_sem=out_sent.at[t], recv_sem=out_got.at[0],
+                        send_sem=out_sent.at[t], recv_sem=out_got.at[t],
                         device_id=place(t, turn(at[t], j), along[t], x_, c_),
                         device_id_type=MESH,
                     ).start()
@@ -253,8 +253,9 @@
         await_bytes(kv.at[t, 0, 0, 0, pl.ds(0, 15)], out_sent.at[t])
         await_bytes(kv.at[t, 0, 0, 0], out_sent.at[t])
 
-    await_bytes(o_got, out_got.at[0])
     for h in range(HEADS):
+        if h % 12 == 0:
+            await_bytes(o_got.at[pl.ds(h, 12)], out_got.at[h // 12])
         conditional, unconditional = o_got[h, 0].astype(F32), o_got[h, 1].astype(F32)
         guided = unconditional + GUIDE * (conditional - unconditional)
         spread[pl.ds(h, 16, stride=HEADS), :] = guided
@@ -264,6 +265,10 @@
 
 
 def local(query_tokens, key_tokens, value_tokens):
+    inputs = [
+        pltpu.with_memory_space_constraint(x, pltpu.HBM)
+        for x in (query_tokens, key_tokens, value_tokens)
+    ]
     anywhere = pl.BlockSpec(memory_space=pltpu.HBM)
     dma = pltpu.SemaphoreType.DMA
     return pl.pallas_call(
@@ -281,14 +286,14 @@
             pltpu.VMEM((2, 2, 16, 16, HD), BF16),
             pltpu.VMEM((HEADS, 2, 16, HD), BF16),
             pltpu.VMEM((32 * HEADS, HD), F32),
-            dma((2,)), dma((2,)), dma((2,)), dma((2, RING, 2)), dma((2, RING, 2)), dma((1,)),
+            dma((2,)), dma((2,)), dma((2,)), dma((2, RING, 2)), dma((2, RING, 2)), dma((2,)),
             dma((2,)), dma((2, 2)), dma((2,)), dma((2,)), dma((2,)),
         ],
         compiler_params=pltpu.CompilerParams(
-            collective_id=0, has_side_effects=True, vmem_limit_bytes=64 * 2**20 - 2**16
+            collective_id=0, has_side_effects=True, vmem_limit_bytes=48 << 20
         ),
         name="guided_attention",
-    )(query_tokens, key_tokens, value_tokens)
+    )(*inputs)
 
 
 def solution(mesh):

time: 51.1 us -> 49 us (0.959)
  local copies, waits for them, and re-layouts: 1.62 us -> 0.68 us
  Pallas kernels: 49 us -> 48.2 us
    unnamed x1, local copies, waits for them, and re-layouts: 1.62 us -> 0.68 us
    pallas_call x1, Pallas kernels: 49 us -> 48.2 us  [local(): pl.pallas_call(kernel, out_shape=jax.ShapeDtypeStruct((32, HEADS, HD // 2...]
where the time goes in v3:
time: 49 us; the launch traced here: 48.9 us
  Pallas kernels  48.2 us (98%)
  local copies, waits for them, and re-layouts  0.68 us (1%)
    pallas_call x1, Pallas kernels, local(): pl.pallas_call(kernel, out_shape=jax.ShapeDtypeStruct((32, HEADS, HD // 2...  48.2 us

profile of v3, /device:TPU:1, one launch (start us, length us, event | category | flops | bytes accessed | tf_op | source)
XLA Modules:
  0.0 48.9 jit_solution(4950875835698297713)
XLA Ops:
  0.0 48.2 %guided_attention.1 = bf16[32,24,64]{2,1,0:T(8,128)(2,1)S(1)} custom-call(bf16[1,32,3072]{2,1,0:T(8,128)(2,1)} %q_in.1, bf16[1,16,3072]{2,1,0:T(8,128)(2,1)} %k_in.1, bf16[1,16,3072]{2,1,0:T(8,128)(2,1)} %v_in.1), custom_call_target="tpu_custom_call" | custom-call | tf_op jit(solution)/shard_map/guided_attention/pallas_call | solution.py:274
  48.2 0.7 %copy.5 = bf16[32,24,64]{2,1,0:T(8,128)(2,1)} copy(bf16[32,24,64]{2,1,0:T(8,128)(2,1)S(1)} %guided_attention.1) | data formatting | bytes 196608

commit v4 on v3

--- a/solution.py
+++ b/solution.py
@@ -147,10 +147,10 @@
         ).start()
 
     def relay(*offsets):
-        for part in range(2):
-            for t in range(2):
-                @pl.when(active[t])
-                def _(t=t, part=part):
+        for t in range(2):
+            @pl.when(active[t])
+            def _(t=t):
+                for part in range(2):
                     for r in offsets:
                         if r != 0:
                             await_bytes(kv.at[t, r, 0, part], ring_got.at[t, r, part])
@@ -158,12 +158,12 @@
                             await_bytes(kv.at[t, 0, 0], kv_got.at[t])
                         pass_on(t, r, part)
 
-    def attend(t, offsets, first):
-        for r in offsets:
+    def attend(t, offsets, first, cores=(0, 1)):
+        for r in offsets if 1 in cores else ():
             for part in range(2):
                 await_bytes(kv.at[t, r, 1, part], core_got.at[t, r, part])
         ones = jnp.ones((256, HD), BF16)
-        chunks = [(r, w) for r in offsets for w in range(2)]
+        chunks = [(r, w) for r in offsets for w in cores]
 
         def score(b):
             rows = q[t, 8 * b : 8 * b + 8].reshape(256, HD)
@@ -212,9 +212,10 @@
     relay(3, 5)
     both(attend, (3, 5), False)
     relay(4)
+    both(attend, (4,), False, (0,))
 
     def finish(t):
-        attend(t, (4,), False)
+        attend(t, (4,), False, (1,))
         whole = acc[t]
         result = (whole[:, :HD] / whole[:, HD:]).reshape(16, 2, 16, HD)
         upper, lower = result[:, 0].reshape(256, HD), result[:, 1].reshape(256, HD)
@@ -238,7 +239,9 @@
                         device_id_type=MESH,
                     ).start()
 
-    both(finish)
+    pl.when(jnp.logical_and(active[0], xl == 1))(functools.partial(finish, 0))
+    pl.when(active[1])(functools.partial(finish, 1))
+    pl.when(jnp.logical_and(active[0], xl == 0))(functools.partial(finish, 0))
 
     for t in range(2):
         await_bytes(kv.at[t, pl.ds(0, 5), 0, 0, pl.ds(0, 8)], a2a_sent.at[t])
@@ -250,9 +253,12 @@
     def drain(t):
         await_bytes(kv.at[t, pl.ds(0, 7), 0], ring_sent.at[t])
         await_bytes(kv.at[t, :, 0], core_sent.at[t])
+
+    def drain_out(t):
         await_bytes(kv.at[t, 0, 0, 0, pl.ds(0, 15)], out_sent.at[t])
         await_bytes(kv.at[t, 0, 0, 0], out_sent.at[t])
 
+    both(drain)
     for h in range(HEADS):
         if h % 12 == 0:
             await_bytes(o_got.at[pl.ds(h, 12)], out_got.at[h // 12])
@@ -261,7 +267,7 @@
         spread[pl.ds(h, 16, stride=HEADS), :] = guided
         spread[pl.ds(16 * HEADS + h, 16, stride=HEADS), :] = pltpu.roll(guided, 64, 1)
     out[...] = spread[...].reshape(32, HEADS, HD)[:, :, : HD // 2].astype(BF16)
-    both(drain)
+    both(drain_out)
 
 
 def local(query_tokens, key_tokens, value_tokens):

time: 49 us -> 48.3 us (0.986)
  Pallas kernels: 48.2 us -> 47.4 us
    pallas_call x1, Pallas kernels: 48.2 us -> 47.4 us  [local(): pl.pallas_call(kernel, out_shape=jax.ShapeDtypeStruct((32, HEADS, HD // 2...]
where the time goes in v4:
time: 48.3 us; the launch traced here: 48.1 us
  Pallas kernels  47.4 us (98%)
  local copies, waits for them, and re-layouts  0.68 us (1%)
    pallas_call x1, Pallas kernels, local(): pl.pallas_call(kernel, out_shape=jax.ShapeDtypeStruct((32, HEADS, HD // 2...  47.4 us

profile of v4, /device:TPU:1, one launch (start us, length us, event | category | flops | bytes accessed | tf_op | source)
XLA Modules:
  0.0 48.1 jit_solution(18316030243383966370)
XLA Ops:
  0.0 47.4 %guided_attention.1 = bf16[32,24,64]{2,1,0:T(8,128)(2,1)S(1)} custom-call(bf16[1,32,3072]{2,1,0:T(8,128)(2,1)} %q_in.1, bf16[1,16,3072]{2,1,0:T(8,128)(2,1)} %k_in.1, bf16[1,16,3072]{2,1,0:T(8,128)(2,1)} %v_in.1), custom_call_target="tpu_custom_call" | custom-call | tf_op jit(solution)/shard_map/guided_attention/pallas_call | solution.py:280
  47.5 0.7 %copy.5 = bf16[32,24,64]{2,1,0:T(8,128)(2,1)} copy(bf16[32,24,64]{2,1,0:T(8,128)(2,1)S(1)} %guided_attention.1) | data formatting | bytes 196608

commit v5 on v4

--- a/solution.py
+++ b/solution.py
@@ -206,11 +206,14 @@
     both(lambda t: await_bytes(q.at[t], q_got.at[t]))
     both(attend, (0,), True)
     relay(1, 7)
-    both(attend, (1, 7), False)
+    both(attend, (1, 7), False, (0,))
+    both(attend, (1, 7), False, (1,))
     relay(2, 6)
-    both(attend, (2, 6), False)
+    both(attend, (2, 6), False, (0,))
+    both(attend, (2, 6), False, (1,))
     relay(3, 5)
-    both(attend, (3, 5), False)
+    both(attend, (3, 5), False, (0,))
+    both(attend, (3, 5), False, (1,))
     relay(4)
     both(attend, (4,), False, (0,))
 

time: 48.3 us -> 48.5 us (level)
  no operation moved by 1% of the time
where the time goes in v5:
time: 48.5 us; the launch traced here: 48.4 us
  Pallas kernels  47.7 us (98%)
  local copies, waits for them, and re-layouts  0.68 us (1%)
    pallas_call x1, Pallas kernels, local(): pl.pallas_call(kernel, out_shape=jax.ShapeDtypeStruct((32, HEADS, HD // 2...  47.7 us

profile of v5, /device:TPU:1, one launch (start us, length us, event | category | flops | bytes accessed | tf_op | source)
XLA Modules:
  0.0 48.4 jit_solution(8223174776497711557)
XLA Ops:
  0.0 47.7 %guided_attention.1 = bf16[32,24,64]{2,1,0:T(8,128)(2,1)S(1)} custom-call(bf16[1,32,3072]{2,1,0:T(8,128)(2,1)} %q_in.1, bf16[1,16,3072]{2,1,0:T(8,128)(2,1)} %k_in.1, bf16[1,16,3072]{2,1,0:T(8,128)(2,1)} %v_in.1), custom_call_target="tpu_custom_call" | custom-call | tf_op jit(solution)/shard_map/guided_attention/pallas_call | solution.py:283
  47.7 0.7 %copy.5 = bf16[32,24,64]{2,1,0:T(8,128)(2,1)} copy(bf16[32,24,64]{2,1,0:T(8,128)(2,1)S(1)} %guided_attention.1) | data formatting | bytes 196608
